TPU v7x, 128 devices: a whole 4x4x4 slice. The times are simulated.
128 devices in a mesh: dp: 4 (over z), row: 8 (over x, core), col: 4 (over y).
Axes of the slice: x: 4, y: 4, z: 4, core: 2. Of those that a mesh axis runs over, the one named last changes fastest.
Arguments:
- activations: bfloat16 [4096, 6144], P(('dp', 'row'), 'col'), parts along dimension 0, may hold values from -6 to 6
- up_weight: bfloat16 [6144, 24576], P('col', 'row'), may hold values from -0.078125 to 0.078125
- down_weight: bfloat16 [24576, 6144], P(('row', 'col')), may hold values from -0.0625 to 0.0625
Outputs:
- ffn_output: bfloat16 [4096, 6144], P(('dp', 'row', 'col')), parts along dimension 0
There are 4 independent parts, one for each index of `dp`. A program takes and returns all parts, laid end to end along the dimension named above; an argument that names none is the same for every part. Nothing has to cross between parts.
All inputs are finite; a program needn't handle non-finite values.
Results may differ from a plain program's by a relative error of at most 0.027.
Values may be sent and summed in bfloat16 or wider, within the bound.
A program may use at most 128 MiB of HBM per device.

v0:
```python
import jax
import jax.numpy as jnp
from jax import lax
from jax.sharding import PartitionSpec as P


def tanh_gelu(values):
    inner = 0.7978845608028654 * (values + 0.044715 * values * values * values)
    return 0.5 * values * (1.0 + jnp.tanh(inner))


def per_device(activations, up_weight, down_weight):
    gathered = lax.all_gather(activations, "row", axis=0, tiled=True)
    summed = lax.psum_scatter(
        lax.dot_general(
            up_weight, gathered, (((0,), (1,)), ((), ())), preferred_element_type=jnp.float32
        ).astype(jnp.bfloat16),
        "col",
        scatter_dimension=0,
        tiled=True,
    ).astype(jnp.float32)
    hidden = tanh_gelu(summed).astype(jnp.bfloat16)
    return lax.psum_scatter(
        lax.dot_general(
            hidden, down_weight, (((0,), (0,)), ((), ())), preferred_element_type=jnp.float32
        ).astype(jnp.bfloat16),
        ("row", "col"),
        scatter_dimension=0,
        tiled=True,
    )


def solution(mesh):
    placed = (P(("dp", "row"), "col"), P("col", "row"), P(("row", "col"), None))
    return jax.shard_map(
        per_device,
        mesh=mesh,
        in_specs=placed,
        out_specs=P(("dp", "row", "col"), None),
        check_vma=False,
    )
```

profile of v0, /device:TPU:0, one launch (start us, length us, event | category | flops | bytes accessed | tf_op | source)
XLA Modules:
  0.0 246.0 jit_solution(9546173785312944758)
XLA Ops:
  6.5 0.0 all-gather.2.cloned.1.call-start
  6.5 0.7 all-gather.2.cloned.1.call-update
  7.3 0.0 reduce-scatter.3.cloned.1.call-start
  7.3 32.0 %all-gather.2.cloned.1.call-done = bf16[1024,1536]{1,0:T(8,128)(2,1)} async-done(((bf16[128,1536]{1,0:T(8,128)(2,1)}), bf16[1024,1536]{1,0:T(8,128)(2,1)}) %all-gather.2.cloned.1.call-update) | async-done | bytes 3145744 | tf_op jit(solution)/shard_map/all_gather | solution.py:13
  39.3 15.3 %convolution_convert_fusion.1 = bf16[3072,1024]{1,0:T(8,128)(2,1)} fusion(bf16[1536,3072]{1,0:T(8,128)(2,1)} %param.4, bf16[1024,1536]{1,0:T(8,128)(2,1)} %all-gather.2.cloned.1.call-done), kind=kOutput, calls=%fused_computation.6 | convolution fusion | flops 9666822144 | bytes 18874368 | tf_op jit(solution)/shard_map/dot_general | solution.py:15
  54.5 0.0 reduce-scatter.3.cloned.1.call-update
  54.6 0.0 reduce-scatter.5.cloned.1.call-start
  54.6 64.1 %reduce-scatter.3.cloned.1.call-done = bf16[768,1024]{1,0:T(8,128)(2,1)} async-done(((bf16[3072,1024]{1,0:T(8,128)(2,1)}), bf16[768,1024]{1,0:T(8,128)(2,1)}) %reduce-scatter.3.cloned.1.call-update) | async-done | bytes 1572880 | tf_op jit(solution)/shard_map/reduce_scatter | solution.py:14
  118.7 16.7 %convolution_convert_fusion = bf16[1024,6144]{1,0:T(8,128)(2,1)} fusion(bf16[768,6144]{1,0:T(8,128)(2,1)} %param.5, bf16[768,1024]{1,0:T(8,128)(2,1)} %reduce-scatter.3.cloned.1.call-done), kind=kOutput, calls=%fused_computation | convolution fusion | flops 9677832192 | bytes 23592960 | tf_op jit(solution)/shard_map/dot_general | solution.py:24
  135.4 0.0 reduce-scatter.5.cloned.1.call-update
  135.4 104.1 %reduce-scatter.5.cloned.1.call-done = bf16[32,6144]{1,0:T(8,128)(2,1)} async-done(((bf16[1024,6144]{1,0:T(8,128)(2,1)}), bf16[32,6144]{1,0:T(8,128)(2,1)}) %reduce-scatter.5.cloned.1.call-update) | async-done | bytes 393232 | tf_op jit(solution)/shard_map/reduce_scatter | solution.py:23
Async XLA Ops:
  6.5 32.7 %all-gather.2.cloned.1.call-start = ((), (), s32[]{:S(2)}) async-start(), calls=%async_computation.2 | async-start | bytes 3538944 | tf_op jit(solution)/shard_map/all_gather | solution.py:13
  7.3 111.5 %reduce-scatter.3.cloned.1.call-start = ((), (), s32[]{:S(2)}) async-start(), calls=%async_computation.3 | async-start | bytes 7864320 | tf_op jit(solution)/shard_map/reduce_scatter | solution.py:14
  54.6 185.0 %reduce-scatter.5.cloned.1.call-start = ((), (), s32[]{:S(2)}) async-start(), calls=%async_computation.4 | async-start | bytes 12976128 | tf_op jit(solution)/shard_map/reduce_scatter | solution.py:23
Sparse Core Ops, SparseCore 0:
  9.0 30.1 all-gather.1
  54.7 64.0 reduce-scatter.2
  135.5 103.9 reduce-scatter.4
where the time goes:
time: 246 us
  waiting for transfers between devices  201 us (82%)
  matrix products  31.9 us (13%)
  between operations  13.1 us (5%)
    reduce_scatter x1, waiting for transfers between devices, per_device(): lax.psum_scatter(lax.dot_general(hidden, down_weight, (((0,), (0,)), ((),...  104 us
    reduce_scatter x1, waiting for transfers between devices, per_device(): lax.psum_scatter(lax.dot_general(up_weight, gathered, (((0,), (1,)), ((),...  64.1 us
    all_gather x1, waiting for transfers between devices, per_device(): gathered = lax.all_gather(activations, 'row', axis=0, tiled=True)  32 us
    dot_general x1, matrix products, per_device(): lax.dot_general(hidden, down_weight, (((0,), (0,)), ((), ())), preferred_...  16.7 us
    dot_general x1, matrix products, per_device(): lax.dot_general(up_weight, gathered, (((0,), (1,)), ((), ())), preferred_...  15.3 us
  transfers between devices with their start and end apart: 3, of which 3 were waited for; matrix products, arithmetic and copies ran while one was open for 0% of the time, Pallas kernels for 0%

commit v1 on v0

v1 whole, which is shorter than its diff:
```python
import functools

import jax
import jax.numpy as jnp
from jax import lax
from jax.experimental import pallas as pl
from jax.experimental.pallas import tpu as pltpu
from jax.sharding import PartitionSpec as P

MESH = pl.DeviceIdType.MESH
F32, BF16 = jnp.float32, jnp.bfloat16
N_X, N_CORE, N_COL = 4, 2, 4
CHUNKS = 8
TILES = 8
UP_SLOTS, DOWN_SLOTS = 3, 2


def tanh_gelu(values):
    inner = 0.7978845608028654 * (values + 0.044715 * values * values * values)
    return 0.5 * values * (1.0 + jnp.tanh(inner))


def wide(ref_value):
    return ref_value.astype(F32)


def kernel(
    act_hbm, up_hbm, down_hbm, out_ref,
    own, act, wu, wd, pu, mid, fin, hid, pd, pr, xm, xf, yt, ys, yr, ot,
    local_sem, wu_sem, wd_sem,
    ag_send, ag_x, ag_p, pu_send, mid_sem, fin_sem, pd_send, pr_sem, x_send, xm_sem, xf_sem, y_send, yr_sem,
):
    dp, row, c = lax.axis_index("dp"), lax.axis_index("row"), lax.axis_index("col")
    x, k = row // N_CORE, row % N_CORE
    rows = act.shape[1] // (N_X * N_CORE)
    half_up = pu.shape[-1]
    tile = wd.shape[-1]
    half = TILES // 2
    group = rows // N_COL

    def device(dx=0, dk=0, dy=0):
        return (dp, lax.rem(x + dx, N_X) * N_CORE + lax.rem(k + dk, N_CORE), lax.rem(c + dy, N_COL))

    right, left, across = device(dx=1), device(dx=3), device(dx=2)
    partner = device(dk=1)
    up_c, down_c, far_c = device(dy=1), device(dy=3), device(dy=2)
    everyone = (right, left, across, partner, up_c, down_c, far_c)

    barrier = pltpu.get_barrier_semaphore()
    for other in everyone:
        pl.semaphore_signal(barrier, inc=1, device_id=other, device_id_type=MESH)

    own_copy = pltpu.make_async_copy(act_hbm, own, local_sem)
    own_copy.start()
    order = (2, 3, 1, 0)

    def wu_copy(g):
        cols = pl.ds(pl.multiple_of(lax.rem(c + order[g], N_COL) * (2 * half_up), 128), 2 * half_up)
        return pltpu.make_async_copy(up_hbm.at[:, cols], wu.at[g], wu_sem.at[g])

    def wd_copy(t):
        return pltpu.make_async_copy(down_hbm.at[:, pl.ds(t * tile, tile)], wd.at[t], wd_sem.at[t])

    for g in range(4):
        wu_copy(g).start()
    for t in range(TILES):
        wd_copy(t).start()

    def send(src, dst, send_sem, recv_sem, to):
        pltpu.make_async_remote_copy(
            src_ref=src, dst_ref=dst, send_sem=send_sem, recv_sem=recv_sem, device_id=to, device_id_type=MESH
        ).start()

    def await_bytes(ref, sem):
        pltpu.make_async_copy(ref, ref, sem).wait()

    def place(core, at_x):
        return pl.ds(pl.multiple_of((core * N_X + at_x) * rows, rows), rows)

    own_copy.wait()
    n_own = rows * CHUNKS
    to_row = lax.broadcasted_iota(jnp.int32, (n_own, n_own), 0)
    from_row = lax.broadcasted_iota(jnp.int32, (n_own, n_own), 1)
    chunk_of, rest = to_row // rows, to_row % rows
    wanted = (rest // group) * (group * CHUNKS) + chunk_of * group + rest % group
    shuffle = jnp.where(from_row == wanted, 1.0, 0.0).astype(BF16)
    shuffled = jnp.dot(shuffle, own[...], preferred_element_type=F32).astype(BF16)
    mine = place(k, x)
    for s in range(CHUNKS):
        act[s, mine, :] = shuffled[s * rows:(s + 1) * rows]

    pl.semaphore_wait(barrier, len(everyone))

    @pl.loop(0, CHUNKS)
    def _(s):
        block = act.at[s, mine]
        send(block, block, ag_send.at[s], ag_x.at[s], right)
        send(block, block, ag_send.at[s], ag_x.at[s], left)
        send(block, block, ag_send.at[s], ag_x.at[s], across)
        send(block, block, ag_send.at[s], ag_p.at[s], partner)

    def forward(s):
        await_bytes(act.at[s, pl.ds(0, 3 * rows)], ag_x.at[s])
        for dx in (1, 3, 2):
            block = act.at[s, place(k, lax.rem(x + dx, N_X))]
            send(block, block, ag_send.at[s], ag_p.at[s], partner)

    def up(s):
        slot = lax.rem(s, UP_SLOTS)

        @pl.when(s >= UP_SLOTS)
        def _():
            await_bytes(pu.at[slot, pl.ds(0, 3)], pu_send.at[slot])

        await_bytes(act.at[s, pl.ds(0, 4 * rows)], ag_p.at[s])
        for g in range(4):
            @pl.when(s == 0)
            def _():
                wu_copy(g).wait()

            part = jnp.dot(act[s], wu[g], preferred_element_type=F32).astype(BF16)
            pu[slot, g, 0] = part[:, :half_up]
            pu[slot, g, 1] = part[:, half_up:]
            if g == 0:
                send(pu.at[slot, 0, 0], mid.at[s, 0], pu_send.at[slot], mid_sem.at[s], down_c)
                send(pu.at[slot, 0, 1], mid.at[s, 1], pu_send.at[slot], mid_sem.at[s], up_c)
            elif g == 1:
                send(pu.at[slot, 1, 1], fin.at[s, 0], pu_send.at[slot], fin_sem.at[s], down_c)
            elif g == 2:
                send(pu.at[slot, 2, 0], fin.at[s, 1], pu_send.at[slot], fin_sem.at[s], up_c)

    def up_mid(s):
        slot = lax.rem(s, UP_SLOTS)
        await_bytes(mid.at[s], mid_sem.at[s])
        pu[slot, 1, 0] = (wide(pu[slot, 1, 0]) + wide(mid[s, 0])).astype(BF16)
        send(pu.at[slot, 1, 0], fin.at[s, 2], pu_send.at[slot], fin_sem.at[s], down_c)
        pu[slot, 2, 1] = (wide(pu[slot, 2, 1]) + wide(mid[s, 1])).astype(BF16)
        send(pu.at[slot, 2, 1], fin.at[s, 3], pu_send.at[slot], fin_sem.at[s], up_c)

    def down(s):
        slot, dslot = lax.rem(s, UP_SLOTS), lax.rem(s, DOWN_SLOTS)
        await_bytes(fin.at[s], fin_sem.at[s])
        first = wide(pu[slot, 3, 0]) + wide(fin[s, 2]) + wide(fin[s, 1])
        hid[:, :half_up] = tanh_gelu(first).astype(BF16)
        second = wide(pu[slot, 3, 1]) + wide(fin[s, 0]) + wide(fin[s, 3])
        hid[:, half_up:] = tanh_gelu(second).astype(BF16)

        @pl.when(s >= DOWN_SLOTS)
        def _():
            await_bytes(pd.at[dslot, 0], pd_send.at[dslot])

        @pl.loop(0, TILES)
        def _(t):
            @pl.when(s == 0)
            def _():
                pltpu.make_async_copy(wd.at[t], wd.at[t], wd_sem.at[t]).wait()

            part = jnp.dot(hid[...], wd[t], preferred_element_type=F32).astype(BF16)
            n = part.shape[0] // 2
            pd[dslot, 0, t] = part[:n]
            pd[dslot, 1, t] = part[n:]
            send(pd.at[dslot, 1 - k, t], pr.at[s, t], pd_send.at[dslot], pr_sem.at[s], partner)

    def rows_of(dx):
        return pl.ds(pl.multiple_of(lax.rem(x + dx, N_X) * rows, rows), rows)

    def pair_sum(s):
        dslot = lax.rem(s, DOWN_SLOTS)
        await_bytes(pr.at[s], pr_sem.at[s])

        @pl.loop(0, TILES)
        def _(t):
            pr[s, t] = (wide(pr[s, t]) + wide(pd[dslot, k, t])).astype(BF16)

        low, high = pl.ds(0, half), pl.ds(half, half)
        send(pr.at[s, low, rows_of(2)], xm.at[s, 0], x_send.at[s], xm_sem.at[s], left)
        send(pr.at[s, high, rows_of(2)], xm.at[s, 1], x_send.at[s], xm_sem.at[s], right)
        send(pr.at[s, high, rows_of(3)], xf.at[s, 0], x_send.at[s], xf_sem.at[s], left)
        send(pr.at[s, low, rows_of(1)], xf.at[s, 1], x_send.at[s], xf_sem.at[s], right)

    def x_mid(s):
        await_bytes(xm.at[s], xm_sem.at[s])
        low, high = pl.ds(0, half), pl.ds(half, half)
        pr[s, low, rows_of(3)] = (wide(pr[s, low, rows_of(3)]) + wide(xm[s, 0])).astype(BF16)
        send(pr.at[s, low, rows_of(3)], xf.at[s, 2], x_send.at[s], xf_sem.at[s], left)
        pr[s, high, rows_of(1)] = (wide(pr[s, high, rows_of(1)]) + wide(xm[s, 1])).astype(BF16)
        send(pr.at[s, high, rows_of(1)], xf.at[s, 3], x_send.at[s], xf_sem.at[s], right)

    def x_end(s):
        await_bytes(xf.at[s], xf_sem.at[s])
        for t in range(TILES):
            total = wide(pr[s, t, rows_of(0)])
            if t < half:
                total = total + wide(xf[s, 2, t]) + wide(xf[s, 1, t])
            else:
                total = total + wide(xf[s, 0, t - half]) + wide(xf[s, 3, t - half])
            q, e = t // 2, t % 2
            for to in range(N_COL):
                yt[to, q * group:(q + 1) * group, e * tile:(e + 1) * tile] = total[to * group:(to + 1) * group]
        for to in range(N_COL):
            ys[s, to] = yt[to].astype(BF16)
        send(ys.at[s, lax.rem(c + 2, N_COL)], yr.at[s, 0], y_send.at[s], yr_sem.at[s], far_c)
        send(ys.at[s, lax.rem(c + 1, N_COL)], yr.at[s, 1], y_send.at[s], yr_sem.at[s], up_c)
        send(ys.at[s, lax.rem(c + 3, N_COL)], yr.at[s, 2], y_send.at[s], yr_sem.at[s], down_c)

    def y_end(s):
        await_bytes(yr.at[s], yr_sem.at[s])
        ot[s] = wide(ys[s, c]) + wide(yr[s, 0]) + wide(yr[s, 1]) + wide(yr[s, 2])

    forward(0)

    @pl.loop(0, CHUNKS + 4)
    def _(i):
        @pl.when((i >= 2) & (i < CHUNKS + 2))
        def _():
            pair_sum(i - 2)

        @pl.when(i < CHUNKS)
        def _():
            up(i)

        @pl.when(i + 1 < CHUNKS)
        def _():
            forward(i + 1)

        @pl.when((i >= 3) & (i < CHUNKS + 3))
        def _():
            x_end(i - 3)

        @pl.when((i >= 1) & (i < CHUNKS + 1))
        def _():
            down(i - 1)

        @pl.when(i < CHUNKS)
        def _():
            up_mid(i)

        @pl.when((i >= 2) & (i < CHUNKS + 2))
        def _():
            x_mid(i - 2)

        @pl.when(i >= 4)
        def _():
            y_end(i - 4)

    wide_cols = ot.shape[-1]
    for s in range(CHUNKS):
        for q in range(N_COL):
            own_out = ot[s, q * group:(q + 1) * group, :]
            yt_rows = slice((s * group) % (4 * group), (s * group) % (4 * group) + group)
            yt[q, yt_rows, :] = own_out
        if s % 4 == 3:
            for q in range(N_COL):
                out_ref[pl.ds((s // 4) * 4 * group, 4 * group), q * wide_cols:(q + 1) * wide_cols] = yt[q].astype(BF16)

    for slot in range(UP_SLOTS):
        await_bytes(pu.at[slot, pl.ds(0, 3)], pu_send.at[slot])
    for slot in range(DOWN_SLOTS):
        await_bytes(pd.at[slot, 0], pd_send.at[slot])

    @pl.loop(0, CHUNKS)
    def _(s):
        await_bytes(act.at[s, pl.ds(0, 7 * rows)], ag_send.at[s])
        await_bytes(pr.at[s, pl.ds(0, 6)], x_send.at[s])
        await_bytes(ys.at[s, pl.ds(0, 3)], y_send.at[s])


def per_device(activations, up_weight, down_weight):
    n_own, depth = activations.shape
    ff_row = up_weight.shape[1]
    ff_own, width = down_weight.shape
    half_up = ff_row // N_COL // 2
    rows = n_own // CHUNKS
    tokens = rows * N_X * N_CORE
    tile = width // TILES
    dma, vmem = pltpu.SemaphoreType.DMA, pltpu.VMEM
    return pl.pallas_call(
        kernel,
        name="fused_feed_forward",
        out_shape=jax.ShapeDtypeStruct((n_own // N_COL, width), BF16),
        in_specs=[pl.BlockSpec(memory_space=pl.ANY)] * 3,
        out_specs=pl.BlockSpec(memory_space=pltpu.VMEM),
        scratch_shapes=[
            vmem((n_own, depth), BF16),
            vmem((CHUNKS, tokens, depth), BF16),
            vmem((4, depth, 2 * half_up), BF16),
            vmem((TILES, ff_own, tile), BF16),
            vmem((UP_SLOTS, 4, 2, tokens, half_up), BF16),
            vmem((CHUNKS, 2, tokens, half_up), BF16),
            vmem((CHUNKS, 4, tokens, half_up), BF16),
            vmem((tokens, ff_own), BF16),
            vmem((DOWN_SLOTS, 2, TILES, tokens // 2, tile), BF16),
            vmem((CHUNKS, TILES, tokens // 2, tile), BF16),
            vmem((CHUNKS, 2, TILES // 2, rows, tile), BF16),
            vmem((CHUNKS, 4, TILES // 2, rows, tile), BF16),
            vmem((N_COL, rows, 2 * tile), F32),
            vmem((CHUNKS, N_COL, rows, 2 * tile), BF16),
            vmem((CHUNKS, 3, rows, 2 * tile), BF16),
            vmem((CHUNKS, rows, 2 * tile), F32),
            dma, dma((4,)), dma((TILES,)),
            dma((CHUNKS,)), dma((CHUNKS,)), dma((CHUNKS,)),
            dma((UP_SLOTS,)), dma((CHUNKS,)), dma((CHUNKS,)),
            dma((DOWN_SLOTS,)), dma((CHUNKS,)),
            dma((CHUNKS,)), dma((CHUNKS,)), dma((CHUNKS,)),
            dma((CHUNKS,)), dma((CHUNKS,)),
        ],
        compiler_params=pltpu.CompilerParams(
            collective_id=0, has_side_effects=True, vmem_limit_bytes=60 * 2**20
        ),
    )(activations, up_weight, down_weight)


def solution(mesh):
    placed = (P(("dp", "row"), "col"), P("col", "row"), P(("row", "col"), None))
    return jax.shard_map(
        per_device,
        mesh=mesh,
        in_specs=placed,
        out_specs=P(("dp", "row", "col"), None),
        check_vma=False,
    )
```

time: 246 us -> 103 us (0.42)
  waiting for transfers between devices: 201 us -> 0 us
  Pallas kernels: 0 us -> 101 us
  matrix products: 31.9 us -> 0 us
  between operations: 13.1 us -> 0.01 us
    reduce_scatter x2 -> x0, waiting for transfers between devices: 168 us -> none  [the longest x1 104 us: per_device(): lax.psum_scatter(lax.dot_general(hidden, down_weight, (((0,), (0,)), ((),...]
    pallas_call x0 -> x1, Pallas kernels: none -> 101 us  [per_device(): pl.pallas_call(kernel, name='fused_feed_forward', out_shape=jax.ShapeDtyp...]
    all_gather x1 -> x0, waiting for transfers between devices: 32 us -> none  [per_device(): gathered = lax.all_gather(activations, 'row', axis=0, tiled=True)]
    dot_general x2 -> x0, matrix products: 31.9 us -> none  [the longest x1 16.7 us: per_device(): lax.dot_general(hidden, down_weight, (((0,), (0,)), ((), ())), preferred_...]
  transfers between devices with their start and end apart: 3 -> 0, of which waited for: 3 -> 0; matrix products, arithmetic and copies ran while one was open for 0% -> 0% of each run, Pallas kernels for 0% -> 0%
where the time goes in v1:
time: 103 us
  Pallas kernels  101 us (98%)
  local copies, waits for them, and re-layouts  1.77 us (2%)
    pallas_call x1, Pallas kernels, per_device(): pl.pallas_call(kernel, name='fused_feed_forward', out_shape=jax.ShapeDtyp...  101 us

profile of v1, /device:TPU:0, one launch (start us, length us, event | category | flops | bytes accessed | tf_op | source)
XLA Modules:
  0.0 103.0 jit_solution(10509306596218458324)
XLA Ops:
  0.0 101.2 %fused_feed_forward.1 = bf16[32,6144]{1,0:T(8,128)(2,1)} custom-call(bf16[128,1536]{1,0:T(8,128)(2,1)} %act_hbm.1, bf16[1536,3072]{1,0:T(8,128)(2,1)} %up_hbm.1, bf16[768,6144]{1,0:T(8,128)(2,1)} %down_hbm.1), custom_call_target="tpu_custom_call" | custom-call | tf_op jit(solution)/shard_map/fused_feed_forward/pallas_call | solution.py:277
  101.2 1.8 %copy.5 = bf16[32,6144]{1,0:T(8,128)(2,1)} copy(bf16[32,6144]{1,0:T(8,128)(2,1)} %fused_feed_forward.1) | data formatting | bytes 786432

commit v2 on v1

v2 whole, which is shorter than its diff:
```python
import functools

import jax
import jax.numpy as jnp
from jax import lax
from jax.experimental import pallas as pl
from jax.experimental.pallas import tpu as pltpu
from jax.sharding import PartitionSpec as P

MESH = pl.DeviceIdType.MESH
F32, BF16 = jnp.float32, jnp.bfloat16
N_X, N_CORE, N_COL = 4, 2, 4
CHUNKS = 8
TILES = 8
UP_SLOTS, DOWN_SLOTS = 4, 3
GATHER_DIRECT, RESULT_DIRECT = (0,), (6, 7)
COL_FIRST = ((6, 0), (6, 1))
ORDER = (
    "G0 G1 G2 H0", "F0 H1 H2 G3", "U0 V0 F1 R0", "U1 F2 H3 G4", "A0 G5 G6 V1", "U2 V2 R1 F3",
    "H4 A1 H5 U3", "D0 H6 E0 F4", "V3 P0 G7 A2", "R2 R3 Q0 U4", "D1 E1 Q1 B0", "H7 F5 C0 P1",
    "V4 A3 S1 D2", "E2 C1 U5 P2", "Q2 F6 V5 A4", "S2 R4 D3 F7", "A5 R5 E3 S0", "B2 U6 P3 V6",
    "Q3 D4 R6 C2", "U7 E4 S3 P4", "V7 Q4 D5 C3", "A6 x1 B3 R7", "E5 P5 B1 A7", "x0 Q5 S5 X3",
    "X2 C4 D6 X0", "B5 E6 C5 x2", "x3 P6 S4 z1", "X1 D7 Q6 E7", "S6 B4 X5 Q7", "P7 x5 x4 Z3",
    "S7 C6 Z1 X4", "B6 z3 Z0 z2", "Z5 z0 C7 B7", "z5 Z2 Z4 z4", "x7 x6 Y1 X6", "z7 X7 Z7 Y2",
    "Y3 Z6 Y5 Y4", "z6 Y6 Y0 Y7",
)


def tanh_gelu(values):
    inner = 0.7978845608028654 * (values + 0.044715 * values * values * values)
    return 0.5 * values * (1.0 + jnp.tanh(inner))


def wide(ref_value):
    return ref_value.astype(F32)


def kernel(
    act_hbm, up_hbm, down_hbm, out_ref,
    own, act, wu, wd, pu, mid, fin, hid, pd, pr, xm, xf, yt, ys, ym, yr, ot, ob,
    local_sem, wu_sem, wd_sem,
    ag_send, ag_x, ag_far, ag_p, pu_send, mid_sem, fin_sem, pd_send, pr_sem, x_send, xm_sem, xf_sem, y_send, ym_sem, yr_sem, out_sem,
):
    dp, row, c = lax.axis_index("dp"), lax.axis_index("row"), lax.axis_index("col")
    x, k = row // N_CORE, row % N_CORE
    rows = act.shape[1] // (N_X * N_CORE)
    half_up = pu.shape[-1]
    tile = wd.shape[-1]
    half = TILES // 2
    group = rows // N_COL

    def device(dx=0, dk=0, dy=0):
        return (dp, lax.rem(x + dx, N_X) * N_CORE + lax.rem(k + dk, N_CORE), lax.rem(c + dy, N_COL))

    right, left, across = device(dx=1), device(dx=3), device(dx=2)
    partner = device(dk=1)
    up_c, down_c, far_c = device(dy=1), device(dy=3), device(dy=2)
    everyone = (right, left, across, partner, up_c, down_c, far_c)

    barrier = pltpu.get_barrier_semaphore()
    for other in everyone:
        pl.semaphore_signal(barrier, inc=1, device_id=other, device_id_type=MESH)

    own_copy = pltpu.make_async_copy(act_hbm, own, local_sem)
    own_copy.start()
    order = (2, 3, 1, 0)

    def wu_copy(g):
        cols = pl.ds(pl.multiple_of(lax.rem(c + order[g], N_COL) * (2 * half_up), 128), 2 * half_up)
        return pltpu.make_async_copy(up_hbm.at[:, cols], wu.at[g], wu_sem.at[g])

    def wd_copy(t):
        return pltpu.make_async_copy(down_hbm.at[:, pl.ds(t * tile, tile)], wd.at[t], wd_sem.at[t])

    def send(src, dst, send_sem, recv_sem, to):
        pltpu.make_async_remote_copy(
            src_ref=src, dst_ref=dst, send_sem=send_sem, recv_sem=recv_sem, device_id=to, device_id_type=MESH
        ).start()

    def await_bytes(ref, sem):
        pltpu.make_async_copy(ref, ref, sem).wait()

    def place(core, at_x):
        return pl.ds(pl.multiple_of((core * N_X + at_x) * rows, rows), rows)

    own_copy.wait()
    for g in range(4):
        wu_copy(g).start()
    n_own = rows * CHUNKS
    to_row = lax.broadcasted_iota(jnp.int32, (n_own, n_own), 0)
    from_row = lax.broadcasted_iota(jnp.int32, (n_own, n_own), 1)
    chunk_of, rest = to_row // rows, to_row % rows
    wanted = (rest // group) * (group * CHUNKS) + chunk_of * group + rest % group
    shuffle = jnp.where(from_row == wanted, 1.0, 0.0).astype(BF16)
    shuffled = jnp.dot(shuffle, own[...], preferred_element_type=F32).astype(BF16)
    mine = place(k, x)
    for s in range(CHUNKS):
        act[s, mine, :] = shuffled[s * rows:(s + 1) * rows]

    pl.semaphore_wait(barrier, len(everyone))

    def gather(s):
        block = act.at[s, mine]
        send(block, block, ag_send.at[s], ag_x.at[s], right)
        send(block, block, ag_send.at[s], ag_x.at[s], left)
        if s in GATHER_DIRECT:
            send(block, block, ag_send.at[s], ag_far.at[s], across)
        send(block, block, ag_send.at[s], ag_p.at[s], partner)

    def relay(s):
        await_bytes(act.at[s, pl.ds(0, 2 * rows)], ag_x.at[s])
        from_left, from_right = (act.at[s, place(k, lax.rem(x + dx, N_X))] for dx in (3, 1))
        cut = act.shape[-1] // 2
        if s not in GATHER_DIRECT:
            send(from_left.at[:, :cut], from_left.at[:, :cut], ag_send.at[s], ag_far.at[s], right)
            send(from_right.at[:, cut:], from_right.at[:, cut:], ag_send.at[s], ag_far.at[s], left)
        send(from_left, from_left, ag_send.at[s], ag_p.at[s], partner)
        send(from_right, from_right, ag_send.at[s], ag_p.at[s], partner)

    def forward(s):
        await_bytes(act.at[s, pl.ds(0, rows)], ag_far.at[s])
        block = act.at[s, place(k, lax.rem(x + 2, N_X))]
        send(block, block, ag_send.at[s], ag_p.at[s], partner)

    def up(s):
        slot = s % UP_SLOTS
        if s >= UP_SLOTS:
            await_bytes(pu.at[slot, pl.ds(0, 3)], pu_send.at[slot])

        await_bytes(act.at[s, pl.ds(0, 4 * rows)], ag_p.at[s])
        up_group(s, 0)
        send(pu.at[slot, 0, 0], mid.at[s, 0], pu_send.at[slot], mid_sem.at[s], down_c)
        send(pu.at[slot, 0, 1], mid.at[s, 1], pu_send.at[slot], mid_sem.at[s], up_c)

    def up_group(s, g):
        slot = s % UP_SLOTS
        if s == 0:
            wu_copy(g).wait()
        part = jnp.dot(act[s], wu[g], preferred_element_type=F32).astype(BF16)
        pu[slot, g, 0] = part[:, :half_up]
        pu[slot, g, 1] = part[:, half_up:]

    def up_rest(s):
        for g in range(1, 4):
            up_group(s, g)
        if s == 0:
            for t in range(TILES):
                wd_copy(t).start()

    def up_raws(s):
        slot = s % UP_SLOTS
        send(pu.at[slot, 1, 1], fin.at[s, 0], pu_send.at[slot], fin_sem.at[s], down_c)
        send(pu.at[slot, 2, 0], fin.at[s, 1], pu_send.at[slot], fin_sem.at[s], up_c)

    def up_mid(s):
        slot = s % UP_SLOTS
        await_bytes(mid.at[s], mid_sem.at[s])
        pu[slot, 1, 0] = (wide(pu[slot, 1, 0]) + wide(mid[s, 0])).astype(BF16)
        send(pu.at[slot, 1, 0], fin.at[s, 2], pu_send.at[slot], fin_sem.at[s], down_c)
        pu[slot, 2, 1] = (wide(pu[slot, 2, 1]) + wide(mid[s, 1])).astype(BF16)
        send(pu.at[slot, 2, 1], fin.at[s, 3], pu_send.at[slot], fin_sem.at[s], up_c)

    def gelu(s):
        slot = s % UP_SLOTS
        await_bytes(fin.at[s], fin_sem.at[s])
        first = wide(pu[slot, 3, 0]) + wide(fin[s, 2]) + wide(fin[s, 1])
        hid[:, :half_up] = tanh_gelu(first).astype(BF16)
        second = wide(pu[slot, 3, 1]) + wide(fin[s, 0]) + wide(fin[s, 3])
        hid[:, half_up:] = tanh_gelu(second).astype(BF16)

    def down(s, side):
        dslot = s % DOWN_SLOTS
        if s >= DOWN_SLOTS:
            await_bytes(pd.at[dslot, 0, pl.ds(side * half, half)], pd_send.at[dslot, side])

        @pl.loop(side * half, (side + 1) * half)
        def _(t):
            if s == 0:
                pltpu.make_async_copy(wd.at[t], wd.at[t], wd_sem.at[t]).wait()
            part = jnp.dot(hid[...], wd[t], preferred_element_type=F32).astype(BF16)
            n = part.shape[0] // 2
            pd[dslot, 0, t] = part[:n]
            pd[dslot, 1, t] = part[n:]
            send(pd.at[dslot, 1 - k, t], pr.at[s, t], pd_send.at[dslot, side], pr_sem.at[s, side], partner)

    def swap(s):
        row, col = (lax.broadcasted_iota(jnp.int32, (hid.shape[0],) * 2, axis) for axis in range(2))
        at = row % rows
        source = row // (N_X * rows) * (N_X * rows) + at // group * rows + row // rows % N_X * group + at % group
        select = jnp.where(col == source, 1.0, 0.0).astype(BF16)
        hid[...] = jnp.dot(select, hid[...], preferred_element_type=F32).astype(BF16)

    def down_low(s):
        gelu(s)
        if (s, 0) in COL_FIRST:
            swap(s)
        down(s, 0)

    def down_high(s):
        if ((s, 0) in COL_FIRST) != ((s, 1) in COL_FIRST):
            swap(s)
        down(s, 1)

    def route(s, side):
        along_x, along_y = ((left, right), across, x), ((down_c, up_c), far_c, c)
        return (along_y, along_x) if (s, side) in COL_FIRST else (along_x, along_y)

    def rows_of(at, step):
        return pl.ds(pl.multiple_of(lax.rem(at + step, N_X) * rows, rows), rows)

    low, high = pl.ds(0, half), pl.ds(half, half)
    sides = (low, high)

    def pair_sum(s, side):
        dslot = s % DOWN_SLOTS
        await_bytes(pr.at[s, sides[side]], pr_sem.at[s, side])

        @pl.loop(side * half, (side + 1) * half)
        def _(t):
            pr[s, t] = (wide(pr[s, t]) + wide(pd[dslot, k, t])).astype(BF16)

        near, _, at = route(s, side)[0]
        send(pr.at[s, sides[side], rows_of(at, 2)], xm.at[s, side], x_send.at[s], xm_sem.at[s, side], near[side])

    def pair_low(s):
        pair_sum(s, 0)

    def pair_high(s):
        pair_sum(s, 1)

    def x_raws(s):
        for side in range(2):
            near, _, at = route(s, side)[0]
            where = rows_of(at, 1 + 2 * side)
            send(pr.at[s, sides[side], where], xf.at[s, side, 0], x_send.at[s], xf_sem.at[s, side], near[1 - side])

    def x_mid(s, side):
        await_bytes(xm.at[s, side], xm_sem.at[s, side])
        near, _, at = route(s, side)[0]
        where = rows_of(at, 3 - 2 * side)
        pr[s, sides[side], where] = (wide(pr[s, sides[side], where]) + wide(xm[s, side])).astype(BF16)
        send(pr.at[s, sides[side], where], xf.at[s, side, 1], x_send.at[s], xf_sem.at[s, side], near[side])

    def mid_low(s):
        x_mid(s, 0)

    def mid_high(s):
        x_mid(s, 1)

    cuts = (pl.ds(0, tile), pl.ds(tile, tile))

    def x_end(s, side):
        cut = cuts[side]
        await_bytes(xf.at[s, side], xf_sem.at[s, side])
        for e in range(half):
            total = wide(pr[s, side * half + e, rows_of(route(s, side)[0][2], 0)]) + wide(xf[s, side, 0, e]) + wide(xf[s, side, 1, e])
            for to in range(N_COL):
                yt[to, e * group:(e + 1) * group, :] = total[to * group:(to + 1) * group]
        for to in range(N_COL):
            ys[s, to, :, cut] = yt[to].astype(BF16)
        towards, far, at = route(s, side)[1]
        near, other, opposite = (lax.rem(at + step, N_COL) for step in ((3, 1, 2), (1, 3, 2))[side])
        if s not in RESULT_DIRECT:
            send(ys.at[s, opposite, :, cut], ym.at[s, side], y_send.at[s], ym_sem.at[s, side], towards[side])
        send(ys.at[s, other, :, cut], yr.at[s, 0, :, cut], y_send.at[s], yr_sem.at[s], towards[1 - side])
        if s in RESULT_DIRECT:
            send(ys.at[s, near, :, cut], yr.at[s, 1, :, cut], y_send.at[s], yr_sem.at[s], towards[side])
            send(ys.at[s, opposite, :, cut], yr.at[s, 2, :, cut], y_send.at[s], yr_sem.at[s], far)

    def x_end_low(s):
        x_end(s, 0)

    def x_end_high(s):
        x_end(s, 1)

    def y_mid(s, side):
        if s in RESULT_DIRECT:
            return
        towards, _, at = route(s, side)[1]
        near = lax.rem(at + (3, 1)[side], N_COL)
        cut = cuts[side]
        await_bytes(ym.at[s, side], ym_sem.at[s, side])
        ys[s, near, :, cut] = (wide(ys[s, near, :, cut]) + wide(ym[s, side])).astype(BF16)
        send(ys.at[s, near, :, cut], yr.at[s, 1, :, cut], y_send.at[s], yr_sem.at[s], towards[side])

    def y_mid_low(s):
        y_mid(s, 0)

    def y_mid_high(s):
        y_mid(s, 1)

    per_pass = CHUNKS // 2

    def y_end(s):
        n_parts = 3 if s in RESULT_DIRECT else 2
        await_bytes(yr.at[s, pl.ds(0, n_parts)], yr_sem.at[s])
        total = jnp.concatenate([wide(ys[s, route(s, side)[1][2], :, cuts[side]]) for side in range(2)], axis=1)
        for n in range(n_parts):
            total = total + wide(yr[s, n])
        at = (s % per_pass) * group
        for side in range(2):
            for e in range(half):
                t = side * half + e
                part = total[e * group:(e + 1) * group, side * tile:(side + 1) * tile]
                ot[s // per_pass, at:at + group, t * tile:(t + 1) * tile] = part
        finished.append(s)
        for n in range(2):
            if s // per_pass == n and all(n * per_pass + m in finished for m in range(per_pass)):
                ob[n] = ot[n].astype(BF16)
                out_copy(n).start()

    def out_copy(n):
        block = pl.ds(n * per_pass * group, per_pass * group)
        return pltpu.make_async_copy(ob.at[n], out_ref.at[block], out_sem.at[n])

    finished = []
    stages = {
        "G": gather, "H": relay, "F": forward, "U": up, "V": up_rest, "R": up_raws, "A": up_mid,
        "D": down_low, "E": down_high, "P": pair_low, "Q": pair_high, "S": x_raws, "B": mid_low, "C": mid_high,
        "X": x_end_low, "x": x_end_high, "Z": y_mid_low, "z": y_mid_high, "Y": y_end,
    }
    for line in ORDER:
        for step in line.split():
            stages[step[0]](int(step[1:]))

    for slot in range(UP_SLOTS):
        await_bytes(pu.at[slot, pl.ds(0, 3)], pu_send.at[slot])
    for slot in range(DOWN_SLOTS):
        for side in range(2):
            await_bytes(pd.at[slot, 0, sides[side]], pd_send.at[slot, side])

    @pl.loop(0, CHUNKS)
    def _(s):
        await_bytes(act.at[s, pl.ds(0, 7 * rows)], ag_send.at[s])
        await_bytes(pr.at[s, pl.ds(0, 6)], x_send.at[s])
        await_bytes(ys.at[s, pl.ds(0, 3)], y_send.at[s])

    for n in range(2):
        out_copy(n).wait()


def per_device(activations, up_weight, down_weight):
    n_own, depth = activations.shape
    ff_row = up_weight.shape[1]
    ff_own, width = down_weight.shape
    half_up = ff_row // N_COL // 2
    rows = n_own // CHUNKS
    tokens = rows * N_X * N_CORE
    tile = width // TILES
    dma, vmem = pltpu.SemaphoreType.DMA, pltpu.VMEM
    return pl.pallas_call(
        kernel,
        name="fused_feed_forward",
        out_shape=jax.ShapeDtypeStruct((n_own // N_COL, width), BF16),
        in_specs=[pl.BlockSpec(memory_space=pl.ANY)] * 3,
        out_specs=pl.BlockSpec(memory_space=pl.ANY),
        scratch_shapes=[
            vmem((n_own, depth), BF16),
            vmem((CHUNKS, tokens, depth), BF16),
            vmem((4, depth, 2 * half_up), BF16),
            vmem((TILES, ff_own, tile), BF16),
            vmem((UP_SLOTS, 4, 2, tokens, half_up), BF16),
            vmem((CHUNKS, 2, tokens, half_up), BF16),
            vmem((CHUNKS, 4, tokens, half_up), BF16),
            vmem((tokens, ff_own), BF16),
            vmem((DOWN_SLOTS, 2, TILES, tokens // 2, tile), BF16),
            vmem((CHUNKS, TILES, tokens // 2, tile), BF16),
            vmem((CHUNKS, 2, TILES // 2, rows, tile), BF16),
            vmem((CHUNKS, 2, 2, TILES // 2, rows, tile), BF16),
            vmem((N_COL, rows, tile), F32),
            vmem((CHUNKS, N_COL, rows, 2 * tile), BF16),
            vmem((CHUNKS, 2, rows, tile), BF16),
            vmem((CHUNKS, 3, rows, 2 * tile), BF16),
            vmem((2, rows, width), F32),
            vmem((2, rows, width), BF16),
            dma, dma((4,)), dma((TILES,)),
            dma((CHUNKS,)), dma((CHUNKS,)), dma((CHUNKS,)), dma((CHUNKS,)),
            dma((UP_SLOTS,)), dma((CHUNKS,)), dma((CHUNKS,)),
            dma((DOWN_SLOTS, 2)), dma((CHUNKS, 2)),
            dma((CHUNKS,)), dma((CHUNKS, 2)), dma((CHUNKS, 2)),
            dma((CHUNKS,)), dma((CHUNKS, 2)), dma((CHUNKS,)), dma((2,)),
        ],
        compiler_params=pltpu.CompilerParams(
            collective_id=0, has_side_effects=True, vmem_limit_bytes=60 * 2**20
        ),
    )(activations, up_weight, down_weight)


def solution(mesh):
    placed = (P(("dp", "row"), "col"), P("col", "row"), P(("row", "col"), None))
    return jax.shard_map(
        per_device,
        mesh=mesh,
        in_specs=placed,
        out_specs=P(("dp", "row", "col"), None),
        check_vma=False,
    )
```

time: 103 us -> 86.9 us (0.84)
  Pallas kernels: 101 us -> 84.9 us
    pallas_call x1, Pallas kernels: 101 us -> 84.9 us  [per_device(): pl.pallas_call(kernel, name='fused_feed_forward', out_shape=jax.ShapeDtyp...]
where the time goes in v2:
time: 86.9 us; the launch traced here: 86.7 us
  Pallas kernels  84.9 us (98%)
  local copies, waits for them, and re-layouts  1.77 us (2%)
    pallas_call x1, Pallas kernels, per_device(): pl.pallas_call(kernel, name='fused_feed_forward', out_shape=jax.ShapeDtyp...  84.9 us
    unnamed x1, local copies, waits for them, and re-layouts  1.77 us

profile of v2, /device:TPU:0, one launch (start us, length us, event | category | flops | bytes accessed | tf_op | source)
XLA Modules:
  0.0 86.7 jit_solution(6593059406371962802)
XLA Ops:
  0.0 84.9 %fused_feed_forward.1 = bf16[32,6144]{1,0:T(8,128)(2,1)} custom-call(bf16[128,1536]{1,0:T(8,128)(2,1)} %act_hbm.1, bf16[1536,3072]{1,0:T(8,128)(2,1)} %up_hbm.1, bf16[768,6144]{1,0:T(8,128)(2,1)} %down_hbm.1), custom_call_target="tpu_custom_call" | custom-call | tf_op jit(solution)/shard_map/fused_feed_forward/pallas_call | solution.py:351
  84.9 1.8 %copy.5 = bf16[32,6144]{1,0:T(8,128)(2,1)} copy(bf16[32,6144]{1,0:T(8,128)(2,1)} %fused_feed_forward.1) | data formatting | bytes 786432

commit v3 on v2

--- a/solution.py
+++ b/solution.py
@@ -101,10 +101,10 @@
 
     def gather(s):
         block = act.at[s, mine]
+        if s in GATHER_DIRECT:
+            send(block, block, ag_send.at[s], ag_far.at[s], across)
         send(block, block, ag_send.at[s], ag_x.at[s], right)
         send(block, block, ag_send.at[s], ag_x.at[s], left)
-        if s in GATHER_DIRECT:
-            send(block, block, ag_send.at[s], ag_far.at[s], across)
         send(block, block, ag_send.at[s], ag_p.at[s], partner)
 
     def relay(s):
@@ -260,12 +260,13 @@
             ys[s, to, :, cut] = yt[to].astype(BF16)
         towards, far, at = route(s, side)[1]
         near, other, opposite = (lax.rem(at + step, N_COL) for step in ((3, 1, 2), (1, 3, 2))[side])
-        if s not in RESULT_DIRECT:
+        if s in RESULT_DIRECT:
+            send(ys.at[s, opposite, :, cut], yr.at[s, 2, :, cut], y_send.at[s], yr_sem.at[s], far)
+        else:
             send(ys.at[s, opposite, :, cut], ym.at[s, side], y_send.at[s], ym_sem.at[s, side], towards[side])
         send(ys.at[s, other, :, cut], yr.at[s, 0, :, cut], y_send.at[s], yr_sem.at[s], towards[1 - side])
         if s in RESULT_DIRECT:
             send(ys.at[s, near, :, cut], yr.at[s, 1, :, cut], y_send.at[s], yr_sem.at[s], towards[side])
-            send(ys.at[s, opposite, :, cut], yr.at[s, 2, :, cut], y_send.at[s], yr_sem.at[s], far)
 
     def x_end_low(s):
         x_end(s, 0)

time: 86.9 us -> 86.9 us (level)
  no operation moved by 1% of the time
where the time goes in v3:
time: 86.9 us; the launch traced here: 86.5 us
  Pallas kernels  84.7 us (97%)
  local copies, waits for them, and re-layouts  1.77 us (2%)
    pallas_call x1, Pallas kernels, per_device(): pl.pallas_call(kernel, name='fused_feed_forward', out_shape=jax.ShapeDtyp...  84.7 us
    unnamed x1, local copies, waits for them, and re-layouts  1.77 us

profile of v3, /device:TPU:0, one launch (start us, length us, event | category | flops | bytes accessed | tf_op | source)
XLA Modules:
  0.0 86.5 jit_solution(2754313215536092767)
XLA Ops:
  0.0 84.7 %fused_feed_forward.1 = bf16[32,6144]{1,0:T(8,128)(2,1)} custom-call(bf16[128,1536]{1,0:T(8,128)(2,1)} %act_hbm.1, bf16[1536,3072]{1,0:T(8,128)(2,1)} %up_hbm.1, bf16[768,6144]{1,0:T(8,128)(2,1)} %down_hbm.1), custom_call_target="tpu_custom_call" | custom-call | tf_op jit(solution)/shard_map/fused_feed_forward/pallas_call | solution.py:352
  84.7 1.8 %copy.5 = bf16[32,6144]{1,0:T(8,128)(2,1)} copy(bf16[32,6144]{1,0:T(8,128)(2,1)} %fused_feed_forward.1) | data formatting | bytes 786432
